TPU v7x, 256 devices: a whole 4x4x8 slice. The times are simulated.
256 devices in a mesh: sp: 64 (over z, y, core), dp: 4 (over x).
Axes of the slice: x: 4, y: 4, z: 8, core: 2. Of those that a mesh axis runs over, the one named last changes fastest.
Arguments:
- queries: bfloat16 [32768, 8192], P(('dp', 'sp')), parts along dimension 0, may hold values from -60 to 60
- key_heads: bfloat16 [32768, 1024], P(('dp', 'sp')), parts along dimension 0, may hold values from -6 to 6
- value_heads: bfloat16 [32768, 1024], P(('dp', 'sp')), parts along dimension 0, may hold values from -6 to 6
- out_grad: bfloat16 [32768, 8192], P(('dp', 'sp')), parts along dimension 0, may hold values from -6 to 6
- segment_ids: int32 [32768], P(('dp', 'sp')), parts along dimension 0, may hold values from 0 to 31, never falling along the last dimension, each value on 1 to 512 neighbouring positions
Outputs:
- d_query: bfloat16 [32768, 8192], P(('dp', 'sp')), parts along dimension 0
- d_key: bfloat16 [32768, 1024], P(('dp', 'sp')), parts along dimension 0
- d_value: bfloat16 [32768, 1024], P(('dp', 'sp')), parts along dimension 0
There are 4 independent parts, one for each index of `dp`. A program takes and returns all parts, laid end to end along the dimension named above; each array names one. Nothing has to cross between parts.
Inputs may be any that keep to these rules, and one draw needn't show every extreme that they name: `segment_ids`: documents are runs of consecutive tokens with rising ids, each of at most 512 tokens; one has exactly 512.
All inputs are finite; a program needn't handle non-finite values.
Results may differ from a plain program's by a relative error of at most 0.0065.
Values may be sent and summed in bfloat16 or wider, within the bound.
No kernel may reach another device: no remote copies, remote signals or barrier semaphores. Data moves between devices by JAX's collectives and lax.ppermute only.
A program may use at most 192 MiB of HBM per device.

v0:
```python
import jax
import jax.numpy as jnp
from jax import lax
from jax.sharding import PartitionSpec as P

HEAD_DIM = 128
MOST = 512


def grad_core(query_part, grad_part, key_part, value_part, allowed, scale):
    scores = (
        jnp.einsum("kgqd,kjd->kgqj", query_part, key_part, preferred_element_type=jnp.float32)
        * scale
    )
    scores = jnp.where(allowed, scores, -1e30)
    row_max = jnp.max(scores, axis=-1, keepdims=True)
    probs = jnp.exp(scores - row_max)
    probs = probs / jnp.sum(probs, axis=-1, keepdims=True)
    probs_low = probs.astype(jnp.bfloat16)
    prob_grads = jnp.einsum(
        "kgqd,kjd->kgqj", grad_part, value_part, preferred_element_type=jnp.float32
    )
    delta = jnp.sum(probs * prob_grads, axis=-1, keepdims=True)
    score_grads = (probs * (prob_grads - delta)).astype(jnp.bfloat16)
    query_grad = (
        jnp.einsum("kgqj,kjd->kgqd", score_grads, key_part, preferred_element_type=jnp.float32)
        * scale
    )
    key_grad = (
        jnp.einsum("kgqj,kgqd->kjd", score_grads, query_part, preferred_element_type=jnp.float32)
        * scale
    )
    value_grad = jnp.einsum(
        "kgqj,kgqd->kjd", probs_low, grad_part, preferred_element_type=jnp.float32
    )
    return (query_grad, key_grad, value_grad)


def body(queries, key_heads, value_heads, out_grad, segment_ids):
    scale = HEAD_DIM ** (-0.5)
    tokens, width = queries.shape
    kv_width = key_heads.shape[1]
    kv_count = kv_width // HEAD_DIM
    group = width // kv_width
    devices = lax.axis_size("sp")
    all_ids = lax.all_gather(segment_ids, "sp", axis=0, tiled=True)
    seq_len = tokens * devices
    local = width // HEAD_DIM // devices
    block = min(512, seq_len)
    span = MOST + block
    keys_wide = jnp.broadcast_to(
        key_heads.reshape(tokens, kv_count, 1, HEAD_DIM), (tokens, kv_count, group, HEAD_DIM)
    ).reshape(tokens, width)
    values_wide = jnp.broadcast_to(
        value_heads.reshape(tokens, kv_count, 1, HEAD_DIM), (tokens, kv_count, group, HEAD_DIM)
    ).reshape(tokens, width)
    moved = (
        lax.all_to_all(queries, "sp", split_axis=1, concat_axis=0, tiled=True),
        lax.all_to_all(out_grad, "sp", split_axis=1, concat_axis=0, tiled=True),
        lax.all_to_all(keys_wide, "sp", split_axis=1, concat_axis=0, tiled=True),
        lax.all_to_all(values_wide, "sp", split_axis=1, concat_axis=0, tiled=True),
    )
    local_q = moved[0].reshape(seq_len, local, HEAD_DIM)
    local_g = moved[1].reshape(seq_len, local, HEAD_DIM)
    filler = jnp.zeros((MOST, local, HEAD_DIM), jnp.bfloat16)
    keys_pad = jnp.concatenate([filler, moved[2].reshape(seq_len, local, HEAD_DIM)], axis=0)
    values_pad = jnp.concatenate([filler, moved[3].reshape(seq_len, local, HEAD_DIM)], axis=0)
    ids_pad = jnp.concatenate([jnp.full((MOST,), -1, jnp.int32), all_ids], axis=0)

    def one_block(carry, number):
        key_acc, value_acc = carry
        start = number * block
        q_blk = lax.dynamic_slice_in_dim(local_q, start, block, 0).transpose(1, 0, 2)[:, None]
        g_blk = lax.dynamic_slice_in_dim(local_g, start, block, 0).transpose(1, 0, 2)[:, None]
        k_win = lax.dynamic_slice_in_dim(keys_pad, start, span, 0).transpose(1, 0, 2)
        v_win = lax.dynamic_slice_in_dim(values_pad, start, span, 0).transpose(1, 0, 2)
        ids_q = lax.dynamic_slice_in_dim(all_ids, start, block, 0)
        ids_k = lax.dynamic_slice_in_dim(ids_pad, start, span, 0)
        q_pos = start + jnp.arange(block, dtype=jnp.int32)
        k_pos = start - MOST + jnp.arange(span, dtype=jnp.int32)
        allowed = (ids_q[:, None] == ids_k[None, :]) & (k_pos[None, :] <= q_pos[:, None])
        query_grad, key_grad, value_grad = grad_core(q_blk, g_blk, k_win, v_win, allowed, scale)
        old_key = lax.dynamic_slice_in_dim(key_acc, start, span, 0)
        old_value = lax.dynamic_slice_in_dim(value_acc, start, span, 0)
        key_acc = lax.dynamic_update_slice_in_dim(
            key_acc, old_key + key_grad.transpose(1, 0, 2), start, 0
        )
        value_acc = lax.dynamic_update_slice_in_dim(
            value_acc, old_value + value_grad.transpose(1, 0, 2), start, 0
        )
        return ((key_acc, value_acc), query_grad[:, 0].transpose(1, 0, 2).astype(jnp.bfloat16))

    zeros_acc = jnp.zeros((seq_len + MOST, local, HEAD_DIM), jnp.float32)
    (key_acc, value_acc), query_blocks = lax.scan(
        one_block, (zeros_acc, zeros_acc), jnp.arange(seq_len // block, dtype=jnp.int32)
    )
    query_seq = query_blocks.reshape(seq_len, local * HEAD_DIM)
    key_seq = key_acc[MOST:].reshape(seq_len, local * HEAD_DIM)
    value_seq = value_acc[MOST:].reshape(seq_len, local * HEAD_DIM)
    d_query = lax.all_to_all(query_seq, "sp", split_axis=0, concat_axis=1, tiled=True)
    key_back, value_back = (
        lax.all_to_all(key_seq, "sp", split_axis=0, concat_axis=1, tiled=True),
        lax.all_to_all(value_seq, "sp", split_axis=0, concat_axis=1, tiled=True),
    )
    d_key = (
        key_back.reshape(tokens, kv_count, group, HEAD_DIM)
        .sum(axis=2)
        .reshape(tokens, kv_width)
        .astype(jnp.bfloat16)
    )
    d_value = (
        value_back.reshape(tokens, kv_count, group, HEAD_DIM)
        .sum(axis=2)
        .reshape(tokens, kv_width)
        .astype(jnp.bfloat16)
    )
    return (d_query, d_key, d_value)


def solution(mesh):
    placed = (
        P(("dp", "sp"), None),
        P(("dp", "sp"), None),
        P(("dp", "sp"), None),
        P(("dp", "sp"), None),
        P(("dp", "sp")),
    )
    return jax.shard_map(
        body,
        mesh=mesh,
        in_specs=placed,
        out_specs=(P(("dp", "sp"), None), P(("dp", "sp"), None), P(("dp", "sp"), None)),
        check_vma=False,
    )
```

profile of v0, /device:TPU:127, one launch (start us, length us, event | category | flops | bytes accessed | tf_op | source)
XLA Modules:
  0.0 752.5 jit_solution(6425091283107186635)
XLA Ops:
  3.5 11.0 %all-to-all-start.3 = ((bf16[128,64,128]{2,0,1:T(8,128)(2,1)}), bf16[128,64,128]{2,0,1:T(8,128)(2,1)S(1)}, u32[]{:S(2)}, u32[]{:S(2)}) async-start(bf16[128,64,128]{2,0,1:T(8,128)(2,1)} %bitcast.118), calls=%async_computation.3 | async-start | bytes 4194304 | tf_op jit(solution)/shard_map/all_to_all | solution.py:61
  14.6 47.9 %all-to-all-done.3 = bf16[128,64,128]{2,0,1:T(8,128)(2,1)S(1)} async-done(((bf16[128,64,128]{2,0,1:T(8,128)(2,1)}), bf16[128,64,128]{2,0,1:T(8,128)(2,1)S(1)}, u32[]{:S(2)}, u32[]{:S(2)}) %all-to-all-start.3) | async-done | bytes 2097184 | tf_op jit(solution)/shard_map/all_to_all | solution.py:61
  64.3 8.9 %all-to-all-start.1 = ((bf16[128,64,128]{2,0,1:T(8,128)(2,1)}), bf16[128,64,128]{2,0,1:T(8,128)(2,1)}, u32[]{:S(2)}, u32[]{:S(2)}) async-start(bf16[128,64,128]{2,0,1:T(8,128)(2,1)} %bitcast.119), calls=%async_computation.1 | async-start | bytes 4194304 | tf_op jit(solution)/shard_map/all_to_all | solution.py:60
  73.2 4.1 copy.29
  77.3 43.8 %all-to-all-done.1 = bf16[128,64,128]{2,0,1:T(8,128)(2,1)} async-done(((bf16[128,64,128]{2,0,1:T(8,128)(2,1)}), bf16[128,64,128]{2,0,1:T(8,128)(2,1)}, u32[]{:S(2)}, u32[]{:S(2)}) %all-to-all-start.1) | async-done | bytes 2097184 | tf_op jit(solution)/shard_map/all_to_all | solution.py:60
  121.1 8.9 %all-to-all-start = ((bf16[128,64,128]{0,2,1:T(8,128)(2,1)}), bf16[128,64,128]{0,2,1:T(8,128)(2,1)}, u32[]{:S(2)}, u32[]{:S(2)}) async-start(bf16[128,64,128]{0,2,1:T(8,128)(2,1)} %bitcast.117), calls=%async_computation | async-start | bytes 4194304 | tf_op jit(solution)/shard_map/all_to_all | solution.py:58
  130.0 4.1 copy.32
  134.2 43.8 %all-to-all-done = bf16[128,64,128]{0,2,1:T(8,128)(2,1)} async-done(((bf16[128,64,128]{0,2,1:T(8,128)(2,1)}), bf16[128,64,128]{0,2,1:T(8,128)(2,1)}, u32[]{:S(2)}, u32[]{:S(2)}) %all-to-all-start) | async-done | bytes 2097184 | tf_op jit(solution)/shard_map/all_to_all | solution.py:58
  177.9 9.1 %all-to-all-start.2 = ((bf16[128,64,128]{0,2,1:T(8,128)(2,1)}), bf16[128,64,128]{0,2,1:T(8,128)(2,1)}, u32[]{:S(2)}, u32[]{:S(2)}) async-start(bf16[128,64,128]{0,2,1:T(8,128)(2,1)} %bitcast.116), calls=%async_computation.2 | async-start | bytes 4194304 | tf_op jit(solution)/shard_map/all_to_all | solution.py:59
  187.0 77.2 %all-gather = s32[64,1,128]{2,1,0:T(1,128)S(1)} all-gather(s32[1,1,128]{2,1,0:T(1,128)S(1)} %bitcast.128), channel_id=1, replica_groups=mesh['sp'=64,'dp'=4] {'sp'}, dimensions={0}, use_global_device_ids=true | all-gather | bytes 33280 | tf_op jit(solution)/shard_map/all_gather | solution.py:46
  265.9 2.7 concatenate.10
  268.7 3.2 copy.30
  271.9 4.1 copy.33
  276.0 2.2 broadcast_in_dim.19.clone
  278.2 2.2 broadcast_in_dim.19
  280.4 207.0 %while.16 = (s32[]{:T(128)}, f32[8704,1,128]{2,0,1:T(8,128)}, f32[8704,1,128]{2,0,1:T(8,128)}, bf16[16,512,1,128]{3,1,2,0:T(8,128)(2,1)}, s32[16]{0:T(128)S(1)},...) while((s32[]{:T(128)}, f32[8704,1,128]{2,0,1:T(8,128)}, ...), condition=%wide.region_4.5_spmd, body=%wide.region_0.4_spmd.sunk | while | flops 682098688 | bytes 21418300 | solution.py:94
  288.3 2.7 fusion.57
  291.0 2.3 fusion.56
  301.2 2.7 fusion.57
  303.9 2.3 fusion.56
  314.2 2.7 fusion.57
  316.8 2.3 fusion.56
  327.1 2.7 fusion.57
  329.8 2.3 fusion.56
  337.9 2.1 fusion.58
  340.0 2.7 fusion.57
  342.7 2.3 fusion.56
  352.9 2.7 fusion.57
  355.6 2.3 fusion.56
  363.8 2.1 fusion.58
  365.8 2.7 fusion.57
  368.6 2.3 fusion.56
  378.8 2.7 fusion.57
  381.5 2.3 fusion.56
  391.7 2.7 fusion.57
  394.4 2.3 fusion.56
  404.7 2.7 fusion.57
  407.4 2.3 fusion.56
  417.6 2.7 fusion.57
  420.3 2.3 fusion.56
  428.5 2.1 fusion.58
  430.5 2.7 fusion.57
  433.2 2.3 fusion.56
  443.5 2.7 fusion.57
  446.2 2.3 fusion.56
  456.4 2.7 fusion.57
  459.1 2.3 fusion.56
  467.3 2.1 fusion.58
  469.4 2.7 fusion.57
  472.1 2.3 fusion.56
  482.3 2.7 fusion.57
  485.0 2.3 fusion.56
  487.4 9.5 %all-to-all-start.4 = ((bf16[64,128,128]{2,1,0:T(8,128)(2,1)}), bf16[64,128,128]{2,1,0:T(8,128)(2,1)S(1)}, u32[]{:S(2)}, u32[]{:S(2)}) async-start(bf16[64,128,128]{2,1,0:T(8,128)(2,1)} %bitcast.123), calls=%async_computation.4 | async-start | bytes 4194304 | tf_op jit(solution)/shard_map/all_to_all | solution.py:100
  496.9 4.4 slice.6
  501.3 43.6 %all-to-all-done.4 = bf16[64,128,128]{2,1,0:T(8,128)(2,1)S(1)} async-done(((bf16[64,128,128]{2,1,0:T(8,128)(2,1)}), bf16[64,128,128]{2,1,0:T(8,128)(2,1)S(1)}, u32[]{:S(2)}, u32[]{:S(2)}) %all-to-all-start.4) | async-done | bytes 2097184 | tf_op jit(solution)/shard_map/all_to_all | solution.py:100
  544.8 9.0 %all-to-all-start.5 = ((f32[64,128,128]{2,1,0:T(8,128)}), f32[64,128,128]{2,1,0:T(8,128)}, u32[]{:S(2)}, u32[]{:S(2)}) async-start(f32[64,128,128]{2,1,0:T(8,128)} %bitcast.114), calls=%async_computation.5 | async-start | bytes 8388608 | tf_op jit(solution)/shard_map/all_to_all | solution.py:102
  553.9 4.5 slice.7
  558.3 88.6 %all-to-all-done.5 = f32[64,128,128]{2,1,0:T(8,128)} async-done(((f32[64,128,128]{2,1,0:T(8,128)}), f32[64,128,128]{2,1,0:T(8,128)}, u32[]{:S(2)}, u32[]{:S(2)}) %all-to-all-start.5) | async-done | bytes 4194336 | tf_op jit(solution)/shard_map/all_to_all | solution.py:102
  646.9 8.8 %all-to-all-start.6 = ((f32[64,128,128]{2,1,0:T(8,128)}), f32[64,128,128]{2,1,0:T(8,128)}, u32[]{:S(2)}, u32[]{:S(2)}) async-start(f32[64,128,128]{2,1,0:T(8,128)} %bitcast.113), calls=%async_computation.6 | async-start | bytes 8388608 | tf_op jit(solution)/shard_map/all_to_all | solution.py:103
  655.8 3.0 copy.35
  658.7 4.1 copy.38
  662.8 2.7 bitcast_reduce_fusion.1
  666.5 82.3 %all-to-all-done.6 = f32[64,128,128]{2,1,0:T(8,128)} async-done(((f32[64,128,128]{2,1,0:T(8,128)}), f32[64,128,128]{2,1,0:T(8,128)}, u32[]{:S(2)}, u32[]{:S(2)}) %all-to-all-start.6) | async-done | bytes 4194336 | tf_op jit(solution)/shard_map/all_to_all | solution.py:103
  748.8 2.7 bitcast_reduce_fusion
  (177 shorter events, 115.9 us)
Async XLA Ops:
  0.6 1.0 copy-start
  3.5 11.1 %copy-start.2 = (bf16[128,1024]{1,0:T(8,128)(2,1)S(1)}, bf16[128,1024]{1,0:T(8,128)(2,1)}, u32[]{:S(2)}) copy-start(bf16[128,1024]{1,0:T(8,128)(2,1)} %param.8) | copy-start | bytes 786436
  3.5 59.0 %all-to-all-start.3 = ((bf16[128,64,128]{2,0,1:T(8,128)(2,1)}), bf16[128,64,128]{2,0,1:T(8,128)(2,1)S(1)}, u32[]{:S(2)}, u32[]{:S(2)}) async-start(bf16[128,64,128]{2,0,1:T(8,128)(2,1)} %bitcast.118), calls=%async_computation.3 | async-start | bytes 4194304 | tf_op jit(solution)/shard_map/all_to_all | solution.py:61
  64.3 56.8 %all-to-all-start.1 = ((bf16[128,64,128]{2,0,1:T(8,128)(2,1)}), bf16[128,64,128]{2,0,1:T(8,128)(2,1)}, u32[]{:S(2)}, u32[]{:S(2)}) async-start(bf16[128,64,128]{2,0,1:T(8,128)(2,1)} %bitcast.119), calls=%async_computation.1 | async-start | bytes 4194304 | tf_op jit(solution)/shard_map/all_to_all | solution.py:60
  121.1 56.8 %all-to-all-start = ((bf16[128,64,128]{0,2,1:T(8,128)(2,1)}), bf16[128,64,128]{0,2,1:T(8,128)(2,1)}, u32[]{:S(2)}, u32[]{:S(2)}) async-start(bf16[128,64,128]{0,2,1:T(8,128)(2,1)} %bitcast.117), calls=%async_computation | async-start | bytes 4194304 | tf_op jit(solution)/shard_map/all_to_all | solution.py:58
  177.9 9.1 %copy-start.3 = (s32[128]{0:T(128)S(1)}, s32[128]{0:T(128)}, u32[]{:S(2)}) copy-start(s32[128]{0:T(128)} %param.11) | copy-start | bytes 1540
  177.9 94.0 %all-to-all-start.2 = ((bf16[128,64,128]{0,2,1:T(8,128)(2,1)}), bf16[128,64,128]{0,2,1:T(8,128)(2,1)}, u32[]{:S(2)}, u32[]{:S(2)}) async-start(bf16[128,64,128]{0,2,1:T(8,128)(2,1)} %bitcast.116), calls=%async_computation.2 | async-start | bytes 4194304 | tf_op jit(solution)/shard_map/all_to_all | solution.py:59
  487.4 57.5 %all-to-all-start.4 = ((bf16[64,128,128]{2,1,0:T(8,128)(2,1)}), bf16[64,128,128]{2,1,0:T(8,128)(2,1)S(1)}, u32[]{:S(2)}, u32[]{:S(2)}) async-start(bf16[64,128,128]{2,1,0:T(8,128)(2,1)} %bitcast.123), calls=%async_computation.4 | async-start | bytes 4194304 | tf_op jit(solution)/shard_map/all_to_all | solution.py:100
  544.8 102.1 %all-to-all-start.5 = ((f32[64,128,128]{2,1,0:T(8,128)}), f32[64,128,128]{2,1,0:T(8,128)}, u32[]{:S(2)}, u32[]{:S(2)}) async-start(f32[64,128,128]{2,1,0:T(8,128)} %bitcast.114), calls=%async_computation.5 | async-start | bytes 8388608 | tf_op jit(solution)/shard_map/all_to_all | solution.py:102
  646.9 101.9 %all-to-all-start.6 = ((f32[64,128,128]{2,1,0:T(8,128)}), f32[64,128,128]{2,1,0:T(8,128)}, u32[]{:S(2)}, u32[]{:S(2)}) async-start(f32[64,128,128]{2,1,0:T(8,128)} %bitcast.113), calls=%async_computation.6 | async-start | bytes 8388608 | tf_op jit(solution)/shard_map/all_to_all | solution.py:103
  665.6 86.9 %copy-start.1 = (bf16[128,1024]{1,0:T(8,128)(2,1)S(1)}, bf16[128,1024]{1,0:T(8,128)(2,1)}, u32[]{:S(2)}) copy-start(bf16[128,1024]{1,0:T(8,128)(2,1)} %param.9) | copy-start | bytes 786436
where the time goes:
time: 761 us; the launch traced here: 753 us
  waiting for transfers between devices  350 us (46%)
  matrix products  167 us (22%)
  blocking collectives  77.2 us (10%)
  starting transfers between devices  65.3 us (9%)
  local copies, waits for them, and re-layouts  58.7 us (8%)
  other arithmetic  22.5 us (3%)
  loops' own time  10.9 us (1%)
    all_to_all x1, waiting for transfers between devices, body(): lax.all_to_all(key_seq, 'sp', split_axis=0, concat_axis=1, tiled=True)  88.6 us
    all_to_all x1, waiting for transfers between devices, body(): lax.all_to_all(value_seq, 'sp', split_axis=0, concat_axis=1, tiled=True)  82.3 us
    all_gather x1, blocking collectives, body(): all_ids = lax.all_gather(segment_ids, 'sp', axis=0, tiled=True)  77.2 us
    all_to_all x1, waiting for transfers between devices, body(): lax.all_to_all(values_wide, 'sp', split_axis=1, concat_axis=0, tiled=True)  47.9 us
    all_to_all x1, waiting for transfers between devices, body(): lax.all_to_all(keys_wide, 'sp', split_axis=1, concat_axis=0, tiled=True)  43.8 us
    all_to_all x1, waiting for transfers between devices, body(): lax.all_to_all(queries, 'sp', split_axis=1, concat_axis=0, tiled=True)  43.8 us
    all_to_all x1, waiting for transfers between devices, body(): lax.all_to_all(query_seq, 'sp', split_axis=0, concat_axis=1, tiled=True)  43.6 us
    dot_general x16, matrix products, grad_core(): jnp.einsum('kgqj,kgqd->kjd', probs_low, grad_part, preferred_element_type...  43.4 us
  transfers between devices with their start and end apart: 7, of which 6 were waited for; matrix products, arithmetic and copies ran while one was open for 5% of the time, Pallas kernels for 0%

commit v1 on v0

v1 whole, which is shorter than its diff:
```python
import functools

import jax
import jax.numpy as jnp
from jax import lax
from jax.experimental import pallas as pl
from jax.experimental.pallas import tpu as pltpu
from jax.sharding import PartitionSpec as P

D = 128
T = 128
GROUP = 8
NEG = -1e30
CHUNKS = 2
CORE_HEADS = 4
HC = CORE_HEADS // CHUNKS
PAY = HC * 512 + 16
SCALE = D ** -0.5
LOG2E = 1.4426950408889634
NT = (((1,), (1,)), ((), ()))
TN = (((0,), (0,)), ((), ()))
NN = (((1,), (0,)), ((), ()))
F32 = jnp.float32
BF16 = jnp.bfloat16


def rows(start, size, step=128):
    return pl.ds(pl.multiple_of(start, step), size)


def prep_kernel(info, key, value, ids, mine, theirs):
    c = info[0]
    for out, core in ((mine, c), (theirs, 1 - c)):
        for h in range(CORE_HEADS):
            cols = rows((core * CORE_HEADS + h) * D, D)
            out[(2 * h) * T:(2 * h + 1) * T, :] = key[:, cols]
            out[(2 * h + 1) * T:(2 * h + 2) * T, :] = value[:, cols]
        out[2 * CORE_HEADS * T:, :] = jnp.broadcast_to(ids[...].astype(F32), (16, T)).astype(BF16)


def join_kernel(info, mine, other, *outs):
    c = info[0]
    for j, out in enumerate(outs):
        for ht in range(2 * HC):
            src = (j * 2 * HC + ht) * T
            out[rows(ht * 256 + c * T, T), :] = mine[src:src + T, :]
            out[rows(ht * 256 + (1 - c) * T, T), :] = other[src:src + T, :]
        a = mine[2 * CORE_HEADS * T:, :].astype(F32)
        b = other[2 * CORE_HEADS * T:, :].astype(F32)
        row = lax.broadcasted_iota(jnp.int32, (16, T), 0)
        out[HC * 512:, :] = jnp.where(row == c, a, b).astype(BF16)


def main_kernel(info, kvo, kv1, kv2, io, i1, i2, qo, qr, go, gr,
                dqo, dqr, own, out1, out2,
                idrow, nb, bias, kwin, vwin, acc_k, acc_v, qs, gs, ps, ds, dqs):
    c, k = info[0], info[1]

    @pl.when(pl.program_id(0) == 0)
    def _():
        old = jnp.where(k >= 2, i2[0:2, :].astype(F32), -1.0)
        mid = jnp.where(k >= 1, i1[0:2, :].astype(F32), -1.0)
        idrow[0:2, :] = old
        idrow[2:4, :] = mid
        idrow[4:6, :] = io[0:2, :].astype(F32)
        key_at = lax.broadcasted_iota(jnp.int32, (T, T), 0)
        query_at = lax.broadcasted_iota(jnp.int32, (T, T), 1)
        for n in range(2):
            s = c if n == 0 else 1 - c
            mine = idrow[pl.ds(s + 4, 1), :]
            first = jnp.max(jnp.where(lax.broadcasted_iota(jnp.int32, (1, T), 1) == 0, mine, -2.0))
            count = jnp.int32(1)
            for b in range(5):
                keys = idrow[pl.ds(s + b, 1), :]
                same = jnp.transpose(jnp.broadcast_to(keys, (T, T))) == mine
                if b == 4:
                    same = same & (key_at <= query_at)
                else:
                    count = count + (jnp.max(keys) == first).astype(jnp.int32)
                bias[n, b * T:(b + 1) * T, :] = jnp.where(same, 0.0, NEG)
            nb[n] = count

    for at, ref in ((0, kv2), (256, kv1), (512, kvo)):
        kwin[at:at + 256, :] = ref[0:256, :]
        vwin[at:at + 256, :] = ref[256:512, :]
    acc_k[...] = jnp.zeros_like(acc_k)
    acc_v[...] = jnp.zeros_like(acc_v)
    for n, (q, g) in enumerate(((qo, go), (qr, gr))):
        for h in range(GROUP):
            qs[n, h * T:(h + 1) * T, :] = q[:, h * D:(h + 1) * D]
            gs[n, h * T:(h + 1) * T, :] = g[:, h * D:(h + 1) * D]

    def window(n, off, blocks):
        width = blocks * T
        at = rows(off + (5 - blocks) * T, width)
        kw, vw = kwin[at, :], vwin[at, :]
        b1 = bias[n, 640 - width:, :]
        b2 = jnp.concatenate([b1, b1], axis=1)
        for pair in range(GROUP // 2):
            cols = slice(pair * 256, (pair + 1) * 256)
            score = lax.dot_general(kw, qs[n, cols, :], NT, preferred_element_type=F32)
            dp = lax.dot_general(vw, gs[n, cols, :], NT, preferred_element_type=F32)
            score = score * (SCALE * LOG2E) + b2
            e = jnp.exp2(score - jnp.max(score, axis=0, keepdims=True))
            inv = 1.0 / jnp.sum(e, axis=0, keepdims=True)
            delta = jnp.sum(e * dp, axis=0, keepdims=True) * inv
            p = e * inv
            ps[0:width, cols] = p.astype(BF16)
            ds[0:width, cols] = (p * (dp - delta)).astype(BF16)
        dsv = ds[0:width, :]
        acc_v[at, :] += lax.dot_general(ps[0:width, :], gs[n], NN, preferred_element_type=F32)
        acc_k[at, :] += lax.dot_general(dsv, qs[n], NN, preferred_element_type=F32)
        dqs[n] = (lax.dot_general(dsv, kw, TN, preferred_element_type=F32) * SCALE).astype(BF16)

    def half(n, carry):
        off = jnp.where(n == 0, c, 1 - c) * T
        for blocks in range(1, 6):
            @pl.when(nb[n] == blocks)
            def _():
                window(n, off, blocks)
        return carry

    lax.fori_loop(0, 2, half, 0)

    for n, out in enumerate((dqo, dqr)):
        for h in range(GROUP):
            out[:, h * D:(h + 1) * D] = dqs[n, h * T:(h + 1) * T, :]
    for at, ref in ((0, out2), (256, out1), (512, own)):
        ref[0:256, :] = (acc_k[at:at + 256, :] * SCALE).astype(ref.dtype)
        ref[256:512, :] = acc_v[at:at + 256, :].astype(ref.dtype)


def sum_kernel(info, own, b1, b2, mine, theirs):
    c = info[0]
    for out, core in ((mine, c), (theirs, 1 - c)):
        for ht in range(2 * HC):
            at = rows(ht * 256 + core * T, T)
            out[ht * T:(ht + 1) * T, :] = (
                own[at, :] + b1[at, :].astype(F32) + b2[at, :].astype(F32)).astype(BF16)


def last_kernel(info, *refs):
    c = info[0]
    mine, other, (key, value) = refs[:CHUNKS], refs[CHUNKS:2 * CHUNKS], refs[2 * CHUNKS:]
    for part, core in ((mine, c), (other, 1 - c)):
        for j in range(CHUNKS):
            for h in range(HC):
                cols = rows((core * CORE_HEADS + j * HC + h) * D, D)
                key[:, cols] = part[j][(2 * h) * T:(2 * h + 1) * T, :]
                value[:, cols] = part[j][(2 * h + 1) * T:(2 * h + 2) * T, :]


def shape(*dims, dtype=BF16):
    return jax.ShapeDtypeStruct(dims, dtype)


SMEM = pl.BlockSpec(memory_space=pltpu.SMEM)
VMEM = pl.BlockSpec(memory_space=pltpu.VMEM)


def simple(kernel, outs, count, flops=0):
    return pl.pallas_call(
        kernel,
        out_shape=outs,
        in_specs=[SMEM] + [VMEM] * count,
        out_specs=tuple(VMEM for _ in outs),
        compiler_params=pltpu.CompilerParams(vmem_limit_bytes=16 * 1024 * 1024),
    )


def main_call(chunk, info, payload, r1, r2, queries, q_other, out_grad, g_other):
    base = chunk * HC
    kv = pl.BlockSpec((512, T), lambda h, info: (h, 0))
    ids = pl.BlockSpec((16, T), lambda h, info: (HC * 512 // 16, 0))
    own = pl.BlockSpec((T, GROUP * D), lambda h, info: (0, info[0] * CORE_HEADS + base + h))
    other = pl.BlockSpec((T, GROUP * D), lambda h, info: (0, base + h))
    part = pl.BlockSpec((T, GROUP * D), lambda h, info: (0, h))
    return pl.pallas_call(
        main_kernel,
        grid_spec=pltpu.PrefetchScalarGridSpec(
            num_scalar_prefetch=1,
            grid=(HC,),
            in_specs=[kv, kv, kv, ids, ids, ids, own, other, own, other],
            out_specs=[part, part, kv, kv, kv],
            scratch_shapes=[
                pltpu.VMEM((8, T), F32),
                pltpu.SMEM((2,), jnp.int32),
                pltpu.VMEM((2, 640, T), F32),
                pltpu.VMEM((768, D), BF16),
                pltpu.VMEM((768, D), BF16),
                pltpu.VMEM((768, D), F32),
                pltpu.VMEM((768, D), F32),
                pltpu.VMEM((2, 1024, D), BF16),
                pltpu.VMEM((2, 1024, D), BF16),
                pltpu.VMEM((640, 1024), BF16),
                pltpu.VMEM((640, 1024), BF16),
                pltpu.VMEM((2, 1024, D), BF16),
            ],
        ),
        out_shape=[
            shape(T, HC * 1024),
            shape(T, HC * 1024),
            shape(HC * 512, T, dtype=F32),
            shape(HC * 512, T),
            shape(HC * 512, T),
        ],
        compiler_params=pltpu.CompilerParams(
            dimension_semantics=("arbitrary",), vmem_limit_bytes=48 * 1024 * 1024),
        cost_estimate=pl.CostEstimate(
            flops=HC * 2 * 640 * 1024 * 128 * 10 * 2, bytes_accessed=HC * 3 * 1024 * 1024,
            transcendentals=HC * 2 * 640 * 1024),
    )(info, payload, r1, r2, payload, r1, r2, queries, q_other, out_grad, g_other)


def body(queries, key_heads, value_heads, out_grad, segment_ids):
    devices = lax.axis_size("sp")
    me = lax.axis_index("sp")
    c, k = me % 2, me // 2
    info = jnp.stack([c, k]).astype(jnp.int32)
    swap = [(i, i ^ 1) for i in range(devices)]

    def ring(by):
        return [(i, (i + by) % devices) for i in range(devices)]

    def send(x, perm):
        return lax.ppermute(x, "sp", perm)

    side = shape(2 * CORE_HEADS * T + 16, T)
    mine, theirs = simple(prep_kernel, (side, side), 3)(
        info, key_heads, value_heads, segment_ids.reshape(1, T))
    other = send(theirs, swap)
    payloads = simple(join_kernel, (shape(PAY, T),) * CHUNKS, 2)(info, mine, other)
    came = [(send(p, ring(2)), send(p, ring(4))) for p in payloads]
    width = CORE_HEADS * GROUP * D
    start = (1 - c) * width
    q_other = send(lax.dynamic_slice(queries, (0, start), (T, width)), swap)
    g_other = send(lax.dynamic_slice(out_grad, (0, start), (T, width)), swap)

    dq_own, dq_other, kv_mine, kv_other = [], [], [], []
    for j in range(CHUNKS):
        dqo, dqr, own, out1, out2 = main_call(
            j, info, payloads[j], *came[j], queries, q_other, out_grad, g_other)
        dq_own.append(dqo)
        dq_other.append(send(dqr, swap))
        b2 = send(out2, ring(-4))
        b1 = send(out1, ring(-2))
        half = shape(2 * HC * T, T)
        a, b = simple(sum_kernel, (half, half), 3)(info, own, b1, b2)
        kv_mine.append(a)
        kv_other.append(send(b, swap))

    left = jnp.concatenate(dq_own, axis=1)
    right = jnp.concatenate(dq_other, axis=1)
    d_query = jnp.where(
        c == 0, jnp.concatenate([left, right], axis=1), jnp.concatenate([right, left], axis=1))
    out = shape(T, 2 * CORE_HEADS * D)
    d_key, d_value = simple(last_kernel, (out, out), 2 * CHUNKS)(info, *kv_mine, *kv_other)
    return (d_query, d_key, d_value)


def solution(mesh):
    row = P(("dp", "sp"), None)
    return jax.shard_map(
        body,
        mesh=mesh,
        in_specs=(row, row, row, row, P(("dp", "sp"))),
        out_specs=(row, row, row),
        check_vma=False,
    )
```

time: 761 us -> 90.6 us (0.12); the launches traced: 753 us -> 90.4 us
  waiting for transfers between devices: 350 us -> 28.7 us
  matrix products: 167 us -> 0 us
  blocking collectives: 77.2 us -> 0 us
  local copies, waits for them, and re-layouts: 58.7 us -> 4.66 us
  starting transfers between devices: 65.3 us -> 29.9 us
  Pallas kernels: 0 us -> 23.6 us
  other arithmetic: 22.5 us -> 2.79 us
  loops' own time: 10.9 us -> 0 us
    all_to_all x7 -> x0, waiting for transfers between devices: 350 us -> none  [the longest x1 88.6 us: body(): lax.all_to_all(key_seq, 'sp', split_axis=0, concat_axis=1, tiled=True)]
    dot_general x80 -> x0, matrix products: 167 us -> none  [the longest x16 43.4 us: grad_core(): jnp.einsum('kgqj,kgqd->kjd', probs_low, grad_part, preferred_element_type...]
    all_gather x1 -> x0, blocking collectives: 77.2 us -> none  [body(): all_ids = lax.all_gather(segment_ids, 'sp', axis=0, tiled=True)]
    all_to_all x7 -> x0, starting transfers between devices: 65.3 us -> none  [the longest x1 11 us: body(): lax.all_to_all(values_wide, 'sp', split_axis=1, concat_axis=0, tiled=True)]
    ppermute x0 -> x15, starting transfers between devices: none -> 29.9 us  [send(): return lax.ppermute(x, 'sp', perm)]
    ppermute x0 -> x15, waiting for transfers between devices: none -> 28.7 us  [send(): return lax.ppermute(x, 'sp', perm)]
    pallas_call x0 -> x7, Pallas kernels: none -> 23.6 us  [the longest x2 19.6 us: main_call(): pl.pallas_call(main_kernel, grid_spec=pltpu.PrefetchScalarGridSpec(num_sc...]
    unnamed x13 -> x6, local copies, waits for them, and re-layouts: 14.9 us -> 0.01 us
  transfers between devices with their start and end apart: 7 -> 15, of which waited for: 6 -> 7; matrix products, arithmetic and copies ran while one was open for 5% -> 3% of each run, Pallas kernels for 0% -> 26%
where the time goes in v1:
time: 90.6 us; the launch traced here: 90.4 us
  starting transfers between devices  29.9 us (33%)
  waiting for transfers between devices  28.7 us (32%)
  Pallas kernels  23.6 us (26%)
  local copies, waits for them, and re-layouts  4.66 us (5%)
  other arithmetic  2.79 us (3%)
    ppermute x15, starting transfers between devices, send(): return lax.ppermute(x, 'sp', perm)  29.9 us
    ppermute x15, waiting for transfers between devices, send(): return lax.ppermute(x, 'sp', perm)  28.7 us
    pallas_call x2, Pallas kernels, main_call(): pl.pallas_call(main_kernel, grid_spec=pltpu.PrefetchScalarGridSpec(num_sc...  19.6 us
    select_n x1, other arithmetic, body(): jnp.where(c == 0, jnp.concatenate([left, right], axis=1), jnp.concatenate...  2.72 us
    dynamic_slice x1, local copies, waits for them, and re-layouts, body(): q_other = send(lax.dynamic_slice(queries, (0, start), (T, width)), swap)  2.34 us
    dynamic_slice x1, local copies, waits for them, and re-layouts, body(): g_other = send(lax.dynamic_slice(out_grad, (0, start), (T, width)), swap)  2.31 us
  transfers between devices with their start and end apart: 15, of which 7 were waited for; matrix products, arithmetic and copies ran while one was open for 3% of the time, Pallas kernels for 26%

profile of v1, /device:TPU:127, one launch (start us, length us, event | category | flops | bytes accessed | tf_op | source)
XLA Modules:
  0.0 90.4 jit_solution(8778846565848430557)
XLA Ops:
  0.7 0.0 copy-start
  0.7 0.0 copy-start.1
  0.7 0.0 copy-start.2
  0.7 2.3 %constant_dynamic-slice_fusion.1 = bf16[128,4096]{1,0:T(8,128)(2,1)} fusion(bf16[128,8192]{1,0:T(8,128)(2,1)} %qo.3, s32[]{:T(128)S(6)} %select_n.26), kind=kLoop, calls=%fused_computation.3 | loop fusion | bytes 2097156 | tf_op jit(solution)/shard_map/dynamic_slice | solution.py:236
  3.0 0.7 collective-permute-start.3
  3.7 2.3 %constant_dynamic-slice_fusion = bf16[128,4096]{1,0:T(8,128)(2,1)} fusion(bf16[128,8192]{1,0:T(8,128)(2,1)} %go.3, s32[]{:T(128)S(6)} %select_n.26), kind=kLoop, calls=%fused_computation.2 | loop fusion | bytes 2097156 | tf_op jit(solution)/shard_map/dynamic_slice | solution.py:237
  6.0 0.0 collective-permute-start.4
  6.0 0.1 pad_add_fusion.info
  6.1 0.0 copy-done
  6.1 0.0 copy-done.1
  6.1 0.0 copy-done.2
  6.1 0.7 shard_map.76
  6.8 0.6 collective-permute-start
  7.4 1.7 %collective-permute-done.other = bf16[1040,128]{1,0:T(8,128)(2,1)S(1)} collective-permute-done((bf16[1040,128]{1,0:T(8,128)(2,1)S(1)}, bf16[1040,128]{1,0:T(8,128)(2,1)S(1)}, u32[]{:S(2)}, u32[]{:S(2)}) %collective-permute-start) | collective-permute-done | bytes 266272 | tf_op jit(solution)/shard_map/ppermute | solution.py:226
  9.1 0.6 shard_map.77
  9.6 2.6 %collective-permute-start.5 = (bf16[1040,128]{1,0:T(8,128)(2,1)S(1)}, bf16[1040,128]{1,0:T(8,128)(2,1)S(1)}, u32[]{:S(2)}, u32[]{:S(2)}) collective-permute-start(bf16[1040,128]{1,0:T(8,128)(2,1)S(1)} %get-tuple-element.27.kvo.io), channel_id=1, source_target_pairs={{0,8},{4,12},{8,16},{12,20},{16,24},{20,28},{24,32},{28,36},{32,40... | collective-permute-start | bytes 798728 | tf_op jit(solution)/shard_map/ppermute | solution.py:226
  12.2 2.3 %collective-permute-start.6 = (bf16[1040,128]{1,0:T(8,128)(2,1)S(1)}, bf16[1040,128]{1,0:T(8,128)(2,1)S(1)}, u32[]{:S(2)}, u32[]{:S(2)}) collective-permute-start(bf16[1040,128]{1,0:T(8,128)(2,1)S(1)} %get-tuple-element.27.kvo.io), channel_id=1, source_target_pairs={{0,16},{4,20},{8,24},{12,28},{16,32},{20,36},{24,40},{28,44},{32,4... | collective-permute-start | bytes 798728 | tf_op jit(solution)/shard_map/ppermute | solution.py:226
  14.5 1.6 %collective-permute-start.1 = (bf16[1040,128]{1,0:T(8,128)(2,1)S(1)}, bf16[1040,128]{1,0:T(8,128)(2,1)S(1)}, u32[]{:S(2)}, u32[]{:S(2)}) collective-permute-start(bf16[1040,128]{1,0:T(8,128)(2,1)S(1)} %get-tuple-element.25.kvo.io), channel_id=1, source_target_pairs={{0,8},{4,12},{8,16},{12,20},{16,24},{20,28},{24,32},{28,36},{32,40... | collective-permute-start | bytes 798728 | tf_op jit(solution)/shard_map/ppermute | solution.py:226
  16.1 7.0 %collective-permute-done.5.kv1.i1 = bf16[1040,128]{1,0:T(8,128)(2,1)S(1)} collective-permute-done((bf16[1040,128]{1,0:T(8,128)(2,1)S(1)}, bf16[1040,128]{1,0:T(8,128)(2,1)S(1)}, u32[]{:S(2)}, u32[]{:S(2)}) %collective-permute-start.5) | collective-permute-done | bytes 266272 | tf_op jit(solution)/shard_map/ppermute | solution.py:226
  23.2 0.0 collective-permute-start.2
  23.2 1.6 %collective-permute-done.6.kv2.i2 = bf16[1040,128]{1,0:T(8,128)(2,1)S(1)} collective-permute-done((bf16[1040,128]{1,0:T(8,128)(2,1)S(1)}, bf16[1040,128]{1,0:T(8,128)(2,1)S(1)}, u32[]{:S(2)}, u32[]{:S(2)}) %collective-permute-start.6) | collective-permute-done | bytes 266272 | tf_op jit(solution)/shard_map/ppermute | solution.py:226
  24.8 0.0 collective-permute-done.3.qr
  24.8 0.0 collective-permute-done.4.gr
  24.8 9.5 %shard_map.79 = (bf16[128,2048]{1,0:T(8,128)(2,1)S(1)}, bf16[128,2048]{1,0:T(8,128)(2,1)S(1)}, f32[1024,128]{1,0:T(8,128)S(1)}, bf16[1024,128]{1,0:T(8,128)(2,1)S(1)}, bf16[1024,128]{1,0:T(8,128)(2,1)S(1)}) custom-call(s32[2]{0:T(128)S(1)} %pad_add_fusion.info, bf16[1040,128]{1,0:T(8,128)(2,1)S(1)} %get-tuple-element.27.kvo.io, ...), custom_call_target="tpu_custom_call" | custom-call | flops 6710886400 | bytes 6291456 | tf_op jit(solution)/shard_map/pallas_call | solution.py:178
  34.3 8.8 %collective-permute-start.11 = (bf16[1024,128]{1,0:T(8,128)(2,1)S(1)}, bf16[1024,128]{1,0:T(8,128)(2,1)S(1)}, u32[]{:S(2)}, u32[]{:S(2)}) collective-permute-start(bf16[1024,128]{1,0:T(8,128)(2,1)S(1)} %get-tuple-element.36), channel_id=1, source_target_pairs={{0,248},{4,252},{8,0},{12,4},{16,8},{20,12},{24,16},{28,20},{32,24... | collective-permute-start | bytes 786440 | tf_op jit(solution)/shard_map/ppermute | solution.py:226
  43.0 0.0 collective-permute-done.1.kv1.i1
  43.0 0.0 collective-permute-done.2.kv2.i2
  43.0 10.1 %shard_map.78 = (bf16[128,2048]{1,0:T(8,128)(2,1)S(1)}, bf16[128,2048]{1,0:T(8,128)(2,1)}, f32[1024,128]{1,0:T(8,128)S(1)}, bf16[1024,128]{1,0:T(8,128)(2,1)S(1)}, bf16[1024,128]{1,0:T(8,128)(2,1)S(1)}) custom-call(s32[2]{0:T(128)S(1)} %pad_add_fusion.info, bf16[1040,128]{1,0:T(8,128)(2,1)S(1)} %get-tuple-element.25.kvo.io, ...), custom_call_target="tpu_custom_call" | custom-call | flops 6710886400 | bytes 6291456 | tf_op jit(solution)/shard_map/pallas_call | solution.py:178
  53.2 2.4 %collective-permute-start.7 = (bf16[128,2048]{1,0:T(8,128)(2,1)}, bf16[128,2048]{1,0:T(8,128)(2,1)S(1)}, u32[]{:S(2)}, u32[]{:S(2)}) collective-permute-start(bf16[128,2048]{1,0:T(8,128)(2,1)} %get-tuple-element.29), channel_id=1, source_target_pairs={{0,4},{4,0},{8,12},{12,8},{16,20},{20,16},{24,28},{28,24},{32,36},... | collective-permute-start | bytes 1572872 | tf_op jit(solution)/shard_map/ppermute | solution.py:226
  55.5 0.0 collective-permute-start.8
  55.5 0.4 collective-permute-start.12
  56.0 0.0 collective-permute-start.10
  56.0 0.0 collective-permute-done.11.b1
  56.0 6.6 %collective-permute-start.9 = (bf16[1024,128]{1,0:T(8,128)(2,1)S(1)}, bf16[1024,128]{1,0:T(8,128)(2,1)S(1)}, u32[]{:S(2)}, u32[]{:S(2)}) collective-permute-start(bf16[1024,128]{1,0:T(8,128)(2,1)S(1)} %get-tuple-element.32), channel_id=1, source_target_pairs={{0,248},{4,252},{8,0},{12,4},{16,8},{20,12},{24,16},{28,20},{32,24... | collective-permute-start | bytes 786440 | tf_op jit(solution)/shard_map/ppermute | solution.py:226
  62.6 4.0 %collective-permute-done.12.b2 = bf16[1024,128]{1,0:T(8,128)(2,1)S(1)} collective-permute-done((bf16[1024,128]{1,0:T(8,128)(2,1)S(1)}, bf16[1024,128]{1,0:T(8,128)(2,1)S(1)}, u32[]{:S(2)}, u32[]{:S(2)}) %collective-permute-start.12) | collective-permute-done | bytes 262176 | tf_op jit(solution)/shard_map/ppermute | solution.py:226
  66.5 0.6 shard_map.81
  67.2 2.5 %collective-permute-start.14 = (bf16[512,128]{1,0:T(8,128)(2,1)S(1)}, bf16[512,128]{1,0:T(8,128)(2,1)S(1)}, u32[]{:S(2)}, u32[]{:S(2)}) collective-permute-start(bf16[512,128]{1,0:T(8,128)(2,1)S(1)} %get-tuple-element.40), channel_id=1, source_target_pairs={{0,4},{4,0},{8,12},{12,8},{16,20},{20,16},{24,28},{28,24},{32,36},... | collective-permute-start | bytes 393224 | tf_op jit(solution)/shard_map/ppermute | solution.py:226
  69.7 2.5 %collective-permute-done.10.b2 = bf16[1024,128]{1,0:T(8,128)(2,1)S(1)} collective-permute-done((bf16[1024,128]{1,0:T(8,128)(2,1)S(1)}, bf16[1024,128]{1,0:T(8,128)(2,1)S(1)}, u32[]{:S(2)}, u32[]{:S(2)}) %collective-permute-start.10) | collective-permute-done | bytes 262176 | tf_op jit(solution)/shard_map/ppermute | solution.py:226
  72.2 11.0 %collective-permute-done.9.b1 = bf16[1024,128]{1,0:T(8,128)(2,1)S(1)} collective-permute-done((bf16[1024,128]{1,0:T(8,128)(2,1)S(1)}, bf16[1024,128]{1,0:T(8,128)(2,1)S(1)}, u32[]{:S(2)}, u32[]{:S(2)}) %collective-permute-start.9) | collective-permute-done | bytes 262176 | tf_op jit(solution)/shard_map/ppermute | solution.py:226
  83.2 0.6 shard_map.80
  83.8 1.4 %collective-permute-start.13 = (bf16[512,128]{1,0:T(8,128)(2,1)S(1)}, bf16[512,128]{1,0:T(8,128)(2,1)S(1)}, u32[]{:S(2)}, u32[]{:S(2)}) collective-permute-start(bf16[512,128]{1,0:T(8,128)(2,1)S(1)} %get-tuple-element.39), channel_id=1, source_target_pairs={{0,4},{4,0},{8,12},{12,8},{16,20},{20,16},{24,28},{28,24},{32,36},... | collective-permute-start | bytes 393224 | tf_op jit(solution)/shard_map/ppermute | solution.py:226
  85.2 0.0 collective-permute-done.14.refs_3_
  85.2 1.0 %collective-permute-done.13.refs_2_ = bf16[512,128]{1,0:T(8,128)(2,1)S(1)} collective-permute-done((bf16[512,128]{1,0:T(8,128)(2,1)S(1)}, bf16[512,128]{1,0:T(8,128)(2,1)S(1)}, u32[]{:S(2)}, u32[]{:S(2)}) %collective-permute-start.13) | collective-permute-done | bytes 131104 | tf_op jit(solution)/shard_map/ppermute | solution.py:226
  86.2 1.5 %shard_map.82 = (bf16[128,1024]{1,0:T(8,128)(2,1)}, bf16[128,1024]{1,0:T(8,128)(2,1)}) custom-call(s32[2]{0:T(128)S(1)} %pad_add_fusion.info, bf16[512,128]{1,0:T(8,128)(2,1)S(1)} %get-tuple-element.34.refs_0_, bf16[512,128]{1,0:T(8,128)(2,1)S(1)} %get-tuple-element.38.refs_1_, bf16[512,128]{1,0:T(8,128)(2,1)S(1)} %collective-permute-done.13.refs_2_, ...), custom_call_target="tpu_custom_call" | custom-call | tf_op jit(solution)/shard_map/pallas_call | solution.py:257
  87.7 0.0 collective-permute-done.7
  87.7 0.0 collective-permute-done.8
  87.7 2.7 %maximum_select_fusion = bf16[128,8192]{1,0:T(8,128)(2,1)} fusion(bf16[128,2048]{1,0:T(8,128)(2,1)} %collective-permute-done.8, bf16[128,2048]{1,0:T(8,128)(2,1)S(1)} %collective-permute-done.7, bf16[128,2048]{1,0:T(8,128)(2,1)S(1)} %get-tuple-element.28, bf16[128,2048]{1,0:T(8,128)(2,1)S(1)} %get-tuple-element.26, pred[]{:T(512)S(6)} %eq.5), kind=kLoop, calls=%fused_computation | loop fusion | flops 17825792 | bytes 4194305 | tf_op jit(solution)/shard_map/jit(_where)/select_n | solution.py:254
Async XLA Ops:
  0.7 5.4 %copy-start = (bf16[128,1024]{1,0:T(8,128)(2,1)S(1)}, bf16[128,1024]{1,0:T(8,128)(2,1)}, u32[]{:S(2)}) copy-start(bf16[128,1024]{1,0:T(8,128)(2,1)} %key.1) | copy-start | bytes 786436
  0.7 5.4 %copy-start.1 = (bf16[128,1024]{1,0:T(8,128)(2,1)S(1)}, bf16[128,1024]{1,0:T(8,128)(2,1)}, u32[]{:S(2)}) copy-start(bf16[128,1024]{1,0:T(8,128)(2,1)} %value.1) | copy-start | bytes 786436
  0.7 5.4 %copy-start.2 = (s32[128]{0:T(128)S(1)}, s32[128]{0:T(128)}, u32[]{:S(2)}) copy-start(s32[128]{0:T(128)} %param.9) | copy-start | bytes 1540
  3.0 21.7 %collective-permute-start.3 = (bf16[128,4096]{1,0:T(8,128)(2,1)}, bf16[128,4096]{1,0:T(8,128)(2,1)S(1)}, u32[]{:S(2)}, u32[]{:S(2)}) collective-permute-start(bf16[128,4096]{1,0:T(8,128)(2,1)} %constant_dynamic-slice_fusion.1), channel_id=1, source_target_pairs={{0,4},{4,0},{8,12},{12,8},{16,20},{20,16},{24,28},{28,24},{32,36},... | collective-permute-start | bytes 3145736 | tf_op jit(solution)/shard_map/ppermute | solution.py:226
  6.0 18.8 %collective-permute-start.4 = (bf16[128,4096]{1,0:T(8,128)(2,1)}, bf16[128,4096]{1,0:T(8,128)(2,1)}, u32[]{:S(2)}, u32[]{:S(2)}) collective-permute-start(bf16[128,4096]{1,0:T(8,128)(2,1)} %constant_dynamic-slice_fusion), channel_id=1, source_target_pairs={{0,4},{4,0},{8,12},{12,8},{16,20},{20,16},{24,28},{28,24},{32,36},... | collective-permute-start | bytes 3145736 | tf_op jit(solution)/shard_map/ppermute | solution.py:226
  6.8 2.3 %collective-permute-start = (bf16[1040,128]{1,0:T(8,128)(2,1)S(1)}, bf16[1040,128]{1,0:T(8,128)(2,1)S(1)}, u32[]{:S(2)}, u32[]{:S(2)}) collective-permute-start(bf16[1040,128]{1,0:T(8,128)(2,1)S(1)} %get-tuple-element.24), channel_id=1, source_target_pairs={{0,4},{4,0},{8,12},{12,8},{16,20},{20,16},{24,28},{28,24},{32,36},... | collective-permute-start | bytes 798728 | tf_op jit(solution)/shard_map/ppermute | solution.py:226
  9.6 13.5 %collective-permute-start.5 = (bf16[1040,128]{1,0:T(8,128)(2,1)S(1)}, bf16[1040,128]{1,0:T(8,128)(2,1)S(1)}, u32[]{:S(2)}, u32[]{:S(2)}) collective-permute-start(bf16[1040,128]{1,0:T(8,128)(2,1)S(1)} %get-tuple-element.27.kvo.io), channel_id=1, source_target_pairs={{0,8},{4,12},{8,16},{12,20},{16,24},{20,28},{24,32},{28,36},{32,40... | collective-permute-start | bytes 798728 | tf_op jit(solution)/shard_map/ppermute | solution.py:226
  12.2 12.5 %collective-permute-start.6 = (bf16[1040,128]{1,0:T(8,128)(2,1)S(1)}, bf16[1040,128]{1,0:T(8,128)(2,1)S(1)}, u32[]{:S(2)}, u32[]{:S(2)}) collective-permute-start(bf16[1040,128]{1,0:T(8,128)(2,1)S(1)} %get-tuple-element.27.kvo.io), channel_id=1, source_target_pairs={{0,16},{4,20},{8,24},{12,28},{16,32},{20,36},{24,40},{28,44},{32,4... | collective-permute-start | bytes 798728 | tf_op jit(solution)/shard_map/ppermute | solution.py:226
  14.5 28.5 %collective-permute-start.1 = (bf16[1040,128]{1,0:T(8,128)(2,1)S(1)}, bf16[1040,128]{1,0:T(8,128)(2,1)S(1)}, u32[]{:S(2)}, u32[]{:S(2)}) collective-permute-start(bf16[1040,128]{1,0:T(8,128)(2,1)S(1)} %get-tuple-element.25.kvo.io), channel_id=1, source_target_pairs={{0,8},{4,12},{8,16},{12,20},{16,24},{20,28},{24,32},{28,36},{32,40... | collective-permute-start | bytes 798728 | tf_op jit(solution)/shard_map/ppermute | solution.py:226
  23.2 19.9 %collective-permute-start.2 = (bf16[1040,128]{1,0:T(8,128)(2,1)S(1)}, bf16[1040,128]{1,0:T(8,128)(2,1)S(1)}, u32[]{:S(2)}, u32[]{:S(2)}) collective-permute-start(bf16[1040,128]{1,0:T(8,128)(2,1)S(1)} %get-tuple-element.25.kvo.io), channel_id=1, source_target_pairs={{0,16},{4,20},{8,24},{12,28},{16,32},{20,36},{24,40},{28,44},{32,4... | collective-permute-start | bytes 798728 | tf_op jit(solution)/shard_map/ppermute | solution.py:226
  34.3 21.7 %collective-permute-start.11 = (bf16[1024,128]{1,0:T(8,128)(2,1)S(1)}, bf16[1024,128]{1,0:T(8,128)(2,1)S(1)}, u32[]{:S(2)}, u32[]{:S(2)}) collective-permute-start(bf16[1024,128]{1,0:T(8,128)(2,1)S(1)} %get-tuple-element.36), channel_id=1, source_target_pairs={{0,248},{4,252},{8,0},{12,4},{16,8},{20,12},{24,16},{28,20},{32,24... | collective-permute-start | bytes 786440 | tf_op jit(solution)/shard_map/ppermute | solution.py:226
  53.2 34.5 %collective-permute-start.7 = (bf16[128,2048]{1,0:T(8,128)(2,1)}, bf16[128,2048]{1,0:T(8,128)(2,1)S(1)}, u32[]{:S(2)}, u32[]{:S(2)}) collective-permute-start(bf16[128,2048]{1,0:T(8,128)(2,1)} %get-tuple-element.29), channel_id=1, source_target_pairs={{0,4},{4,0},{8,12},{12,8},{16,20},{20,16},{24,28},{28,24},{32,36},... | collective-permute-start | bytes 1572872 | tf_op jit(solution)/shard_map/ppermute | solution.py:226
  55.5 32.2 %collective-permute-start.8 = (bf16[128,2048]{1,0:T(8,128)(2,1)S(1)}, bf16[128,2048]{1,0:T(8,128)(2,1)}, u32[]{:S(2)}, u32[]{:S(2)}) collective-permute-start(bf16[128,2048]{1,0:T(8,128)(2,1)S(1)} %get-tuple-element.30), channel_id=1, source_target_pairs={{0,4},{4,0},{8,12},{12,8},{16,20},{20,16},{24,28},{28,24},{32,36},... | collective-permute-start | bytes 1572872 | tf_op jit(solution)/shard_map/ppermute | solution.py:226
  55.5 11.0 %collective-permute-start.12 = (bf16[1024,128]{1,0:T(8,128)(2,1)S(1)}, bf16[1024,128]{1,0:T(8,128)(2,1)S(1)}, u32[]{:S(2)}, u32[]{:S(2)}) collective-permute-start(bf16[1024,128]{1,0:T(8,128)(2,1)S(1)} %get-tuple-element.37), channel_id=1, source_target_pairs={{0,240},{4,244},{8,248},{12,252},{16,0},{20,4},{24,8},{28,12},{32,... | collective-permute-start | bytes 786440 | tf_op jit(solution)/shard_map/ppermute | solution.py:226
  56.0 16.2 %collective-permute-start.10 = (bf16[1024,128]{1,0:T(8,128)(2,1)S(1)}, bf16[1024,128]{1,0:T(8,128)(2,1)S(1)}, u32[]{:S(2)}, u32[]{:S(2)}) collective-permute-start(bf16[1024,128]{1,0:T(8,128)(2,1)S(1)} %get-tuple-element.33), channel_id=1, source_target_pairs={{0,240},{4,244},{8,248},{12,252},{16,0},{20,4},{24,8},{28,12},{32,... | collective-permute-start | bytes 786440 | tf_op jit(solution)/shard_map/ppermute | solution.py:226
  56.0 27.2 %collective-permute-start.9 = (bf16[1024,128]{1,0:T(8,128)(2,1)S(1)}, bf16[1024,128]{1,0:T(8,128)(2,1)S(1)}, u32[]{:S(2)}, u32[]{:S(2)}) collective-permute-start(bf16[1024,128]{1,0:T(8,128)(2,1)S(1)} %get-tuple-element.32), channel_id=1, source_target_pairs={{0,248},{4,252},{8,0},{12,4},{16,8},{20,12},{24,16},{28,20},{32,24... | collective-permute-start | bytes 786440 | tf_op jit(solution)/shard_map/ppermute | solution.py:226
  67.2 18.1 %collective-permute-start.14 = (bf16[512,128]{1,0:T(8,128)(2,1)S(1)}, bf16[512,128]{1,0:T(8,128)(2,1)S(1)}, u32[]{:S(2)}, u32[]{:S(2)}) collective-permute-start(bf16[512,128]{1,0:T(8,128)(2,1)S(1)} %get-tuple-element.40), channel_id=1, source_target_pairs={{0,4},{4,0},{8,12},{12,8},{16,20},{20,16},{24,28},{28,24},{32,36},... | collective-permute-start | bytes 393224 | tf_op jit(solution)/shard_map/ppermute | solution.py:226
  83.8 2.4 %collective-permute-start.13 = (bf16[512,128]{1,0:T(8,128)(2,1)S(1)}, bf16[512,128]{1,0:T(8,128)(2,1)S(1)}, u32[]{:S(2)}, u32[]{:S(2)}) collective-permute-start(bf16[512,128]{1,0:T(8,128)(2,1)S(1)} %get-tuple-element.39), channel_id=1, source_target_pairs={{0,4},{4,0},{8,12},{12,8},{16,20},{20,16},{24,28},{28,24},{32,36},... | collective-permute-start | bytes 393224 | tf_op jit(solution)/shard_map/ppermute | solution.py:226
